TPU v7x, 256 devices: a whole 4x4x8 slice. The times are simulated.
256 devices in a mesh: seq: 32 (over y, z), head: 8 (over x, core).
Axes of the slice: x: 4, y: 4, z: 8, core: 2. Of those that a mesh axis runs over, the one named last changes fastest.
Arguments:
- queries: bfloat16 [24576, 4096], P('seq', 'head'), may hold values from -120 to 120
- residual: bfloat16 [24576, 8192], P('seq', 'head'), may hold values from -3 to 3
- nbr_kv: bfloat16 [512, 2, 128, 4096], P('seq', None, None, 'head'), may hold values from -12 to 12
- nbr_owner: int32 [384, 2], P('seq'), may hold values from 0 to 31, all different within a row; in each aligned block of 12 rows (0 to 11, 12 to 23, ...) at most 2 rows name the same one
- nbr_slot: int32 [384, 2], P('seq'), may hold values from 0 to 15
- out_weight: bfloat16 [4096, 8192], P('seq', 'head'), may hold values from -0.09375 to 0.09375
Outputs:
- mixed: bfloat16 [24576, 8192], P('seq', 'head')
Inputs may be any that keep to these rules, and one draw needn't show every extreme that they name: `nbr_owner`: the two owners of a block differ. Among the 12 blocks of one index of seq no owner is named more than 2 times, and this is reached.
All inputs are finite; a program needn't handle non-finite values.
Results may differ from a plain program's by a relative error of at most 0.008.
Values may be sent and summed in bfloat16 or wider, within the bound.
No kernel may reach another device: no remote copies, remote signals or barrier semaphores. Data moves between devices by JAX's collectives and lax.ppermute only.
A program may use at most 128 MiB of HBM per device.

v0:
```python
import jax
import jax.numpy as jnp
from jax import lax
from jax.sharding import PartitionSpec as P

HDIM = 128
BLOCK = 64


def from_behind(value, axis, steps):
    count = lax.axis_size(axis)
    leading, last = (max(0, -steps), min(count, count - steps))
    return lax.ppermute(value, axis, [(source, source + steps) for source in range(leading, last)])


def request_table(owners, slot_ids, seq_count, capacity):
    request_count = owners.shape[0]
    positions = jnp.arange(request_count, dtype=jnp.int32)
    same_owner = owners[:, None] == owners[None, :]
    earlier = positions[None, :] < positions[:, None]
    own_rank = jnp.sum((same_owner & earlier).astype(jnp.int32), axis=1)
    target = owners * capacity + own_rank
    places = jnp.arange(seq_count * capacity, dtype=jnp.int32)
    matches = (places[:, None] == target[None, :]).astype(jnp.int32)
    source = jnp.sum(matches * positions[None, :], axis=1)
    filled = jnp.sum(matches, axis=1) > 0
    wanted = jnp.sum(matches * slot_ids[None, :], axis=1)
    return (target, source, filled, wanted)


def score_rows(query_rows, key_rows, head_count):
    query_split = query_rows.reshape(query_rows.shape[:2] + (head_count, HDIM))
    key_split = key_rows.reshape(key_rows.shape[:2] + (head_count, HDIM))
    scores = jnp.einsum(
        "bqhd,bkhd->bhqk", query_split, key_split, preferred_element_type=jnp.float32
    )
    return scores * HDIM ** (-0.5)


def combine_pairs(partial_value, maxes, sums, feat_width):
    joint = jnp.max(maxes, axis=1, keepdims=True)
    factor = jnp.exp(maxes - joint) * sums
    factor = jnp.transpose(factor, (0, 1, 3, 2))[..., None]
    merged = jnp.sum(factor * partial_value.astype(jnp.float32), axis=1) / jnp.sum(factor, axis=1)
    return merged.astype(jnp.bfloat16).reshape(
        partial_value.shape[0], partial_value.shape[2], feat_width
    )


def shards(queries, residual, nbr_kv, nbr_owner, nbr_slot, out_weight):
    tok_rows, feat_width = queries.shape
    head_count = feat_width // HDIM
    shift_rows = BLOCK - 1
    block_count = tok_rows // BLOCK
    pair_count = nbr_owner.shape[1]
    seq_count = lax.axis_size("seq")
    capacity = max(2, 2 * ((pair_count * block_count + seq_count - 1) // seq_count))
    next_rows = from_behind(queries[:shift_rows], "seq", -1)
    extended = jnp.concatenate([queries[shift_rows:], next_rows], axis=0).reshape(
        block_count, BLOCK, feat_width
    )
    target, source, filled, wanted = request_table(
        nbr_owner.reshape(-1), nbr_slot.reshape(-1), seq_count, capacity
    )
    entry_shape = nbr_kv.shape[1:]
    nbr_rows = entry_shape[1]
    slot_total = seq_count * capacity
    slot_ids = lax.all_to_all(
        wanted.reshape(seq_count, capacity), "seq", split_axis=0, concat_axis=0, tiled=True
    )
    picked = jnp.take(nbr_kv, slot_ids.reshape(-1), axis=0)
    picked = picked.reshape(slot_ids.shape + entry_shape)
    arrived = lax.all_to_all(picked, "seq", split_axis=0, concat_axis=0, tiled=True)
    fetched = jnp.take(arrived.reshape((slot_total,) + entry_shape), target, axis=0)
    fetched = fetched.reshape((block_count, pair_count) + entry_shape)
    key_rows = fetched[:, :, 0].reshape(block_count, pair_count * nbr_rows, feat_width)
    value_rows = fetched[:, :, 1].reshape(block_count, pair_count, nbr_rows, head_count, HDIM)
    scores = score_rows(extended, key_rows, head_count)
    scores = scores.reshape(block_count, head_count, BLOCK, pair_count, nbr_rows)
    row_max = jnp.max(scores, axis=-1)
    weights = jnp.exp(scores - row_max[..., None])
    weight_sum = jnp.sum(weights, axis=-1)
    blended = jnp.einsum(
        "bhqjk,bjkhd->bjqhd",
        weights.astype(jnp.bfloat16),
        value_rows,
        preferred_element_type=jnp.float32,
    )
    partial_value = (blended / jnp.transpose(weight_sum, (0, 3, 2, 1))[..., None]).astype(
        jnp.bfloat16
    )
    maxes = jnp.transpose(row_max, (0, 3, 1, 2))
    sums = jnp.transpose(weight_sum, (0, 3, 1, 2))
    attended = combine_pairs(partial_value, maxes, sums, feat_width)
    flat_out = attended.reshape(tok_rows, feat_width)
    carried = from_behind(flat_out[tok_rows - shift_rows :], "seq", 1)
    placed = jnp.concatenate([carried, flat_out[: tok_rows - shift_rows]], axis=0)
    every_head = lax.all_gather(placed, "head", axis=1, tiled=True)
    projected = jnp.dot(
        every_head,
        lax.all_gather(out_weight, "seq", axis=0, tiled=True),
        preferred_element_type=jnp.float32,
    )
    return (residual.astype(jnp.float32) + projected).astype(jnp.bfloat16)


def solution(mesh):
    return jax.shard_map(
        shards,
        mesh=mesh,
        in_specs=(
            P("seq", "head"),
            P("seq", "head"),
            P("seq", None, None, "head"),
            P("seq", None),
            P("seq", None),
            P("seq", "head"),
        ),
        out_specs=P("seq", "head"),
        check_vma=False,
    )
```

profile of v0, /device:TPU:1, one launch (start us, length us, event | category | flops | bytes accessed | tf_op | source)
XLA Modules:
  0.0 642.3 jit_solution(13466424252039056740)
XLA Ops:
  6.5 0.8 copy.97
  7.3 0.1 reshape.118
  7.4 0.2 convert_reduce_fusion
  7.6 0.8 copy.100
  8.4 0.1 mul.52
  8.4 0.1 select_reduce_fusion
  8.5 0.1 all_to_all.9
  8.6 20.5 %all_to_all.14 = s32[32,1,2]{2,1,0:T(1,128)S(1)} all-to-all(s32[32,1,2]{2,1,0:T(1,128)S(1)} %bitcast.54), channel_id=1, replica_groups=mesh['seq'=32,'head'=8] {'seq'}, dimensions={0} | all-to-all | bytes 512 | tf_op jit(solution)/shard_map/all_to_all | solution.py:68
  29.1 0.5 broadcast.117
  29.6 0.7 reduce.8
  30.3 0.1 reshape.120
  30.4 0.1 copy.102
  30.5 0.1 copy.103
  30.6 9.5 %gather_fusion = bf16[64,2,128,512]{3,2,1,0:T(8,128)(2,1)} fusion(bf16[16,2,128,512]{3,2,1,0:T(8,128)(2,1)} %param.8, s32[1024]{0:T(1024)S(1)} %pad_clamp_fusion.1), kind=kCustom, calls=%fused_computation | custom fusion | bytes 33554688 | tf_op jit(solution)/shard_map/jit(_take)/gather | solution.py:71
  40.2 14.2 %broadcast_select_fusion = bf16[32,2,2,128,512]{4,3,2,1,0:T(8,128)(2,1)} fusion(bf16[32,2,2,128,512]{4,3,2,1,0:T(8,128)(2,1)} %bitcast.46, pred[32,2]{1,0:T(8,128)(4,1)S(1)} %copy.103), kind=kLoop, calls=%fused_computation.2 | loop fusion | flops 8388608 | bytes 33554496 | tf_op jit(solution)/shard_map/jit(_take)/select_n | solution.py:71
  54.4 5.3 all-to-all-start.1
  59.7 0.7 all-gather.5.cloned.1.call-update
  60.5 1.5 collective-permute-start
  62.0 0.1 reduce_sum.50
  62.1 0.2 slice.18
  62.3 0.1 copy.104
  62.3 0.1 mul.55
  62.4 0.1 copy.98
  62.5 0.1 copy.99
  62.7 421.1 %collective-permute-done = bf16[63,512]{1,0:T(8,128)(2,1)S(1)} collective-permute-done((bf16[63,512]{1,0:T(8,128)(2,1)S(1)}, bf16[63,512]{1,0:T(8,128)(2,1)S(1)}, u32[]{:S(2)}, u32[]{:S(2)}) %collective-permute-start) | collective-permute-done | bytes 64544 | tf_op jit(solution)/shard_map/ppermute | solution.py:13
  483.8 1.1 reshape_reshape.4
  484.9 6.4 all-to-all-done.1
  491.3 10.2 %gather_fusion.1 = bf16[24,2,128,512]{3,2,1,0:T(8,128)(2,1)} fusion(bf16[64,2,128,512]{3,2,1,0:T(8,128)(2,1)} %bitcast.4, s32[1024]{0:T(1024)S(1)} %pad_clamp_fusion), kind=kCustom, calls=%fused_computation.1 | custom fusion | bytes 12583008 | tf_op jit(solution)/shard_map/jit(_take)/gather | solution.py:74
  501.5 8.6 %copy.105 = bf16[12,2,2,128,512]{3,4,1,0,2:T(8,128)(2,1)} copy(bf16[12,2,2,128,512]{4,3,2,1,0:T(8,128)(2,1)} %bitcast.47) | data formatting | bytes 12582912 | tf_op jit(solution)/shard_map/jit(_take)/gather | solution.py:74
  510.1 3.5 broadcast_select_fusion.1
  513.6 2.1 fusion.19
  515.7 2.8 copy.106
  518.5 3.8 reshape_reshape_squeeze.3
  522.3 4.1 fusion.20
  526.3 3.5 reshape.122
  529.9 4.5 reduce_max.18
  534.4 1.9 copy.109
  536.3 10.4 %fusion.6 = (bf16[12,4,64,2,128]{4,3,2,1,0:T(2,128)(2,1)}, f32[12,4,64,2]{3,2,1,0:T(8,128)}) fusion(f32[12,4,64,2,128]{4,3,2,1,0:T(2,128)S(1)} %reshape.122, f32[12,4,64,2]{3,2,1,0:T(8,128)} %reduce_max.18), kind=kLoop, calls=%fused_computation.12 | loop fusion | flops 2353152 | bytes 4767744 | tf_op jit(solution)/shard_map/convert_element_type | solution.py:85
  546.6 1.9 copy.110
  548.6 6.0 multiply_reduce_fusion
  554.6 0.5 divide_convert_fusion
  555.1 0.6 copy.113
  555.7 0.1 copy.131
  555.9 1.4 collective-permute-start.1
  557.4 1.3 collective-permute-done.1
  558.6 1.0 pad_maximum_fusion.1
  559.8 63.7 %all-gather.3.cloned.1.call-done = bf16[768,4096]{1,0:T(8,128)(2,1)} async-done(((bf16[768,512]{1,0:T(8,128)(2,1)}), bf16[768,4096]{1,0:T(8,128)(2,1)}) %all-gather.3.cloned.1.call-update) | async-done | bytes 6291472 | tf_op jit(solution)/shard_map/all_gather | solution.py:98
  623.4 12.1 %add_convert_fusion = bf16[768,1024]{1,0:T(8,128)(2,1)} fusion(bf16[768,1024]{1,0:T(8,128)(2,1)S(1)} %copy-done.2, bf16[768,4096]{1,0:T(8,128)(2,1)} %all-gather.3.cloned.1.call-done, bf16[4096,1024]{1,0:T(8,128)(2,1)} %all-gather.5.cloned.1.call-done), kind=kOutput, calls=%fused_computation.8 | convolution fusion | flops 6444810240 | bytes 17825792 | tf_op jit(solution)/shard_map/dot_general | solution.py:99
  (23 shorter events, 0.4 us)
Async XLA Ops:
  54.4 6.1 copy-start
  54.4 7.9 %copy-start.1 = (s32[12,2]{0,1:T(2,128)S(1)}, s32[12,2]{0,1:T(2,128)}, u32[]{:S(2)}) copy-start(s32[12,2]{0,1:T(2,128)} %param.9) | copy-start | bytes 292
  54.4 436.9 %all-to-all-start.1 = ((bf16[32,2,2,128,512]{4,3,2,1,0:T(8,128)(2,1)}), bf16[32,2,2,128,512]{4,3,2,1,0:T(8,128)(2,1)}, u32[]{:S(2)}, u32[]{:S(2)}) async-start(bf16[32,2,2,128,512]{4,3,2,1,0:T(8,128)(2,1)} %broadcast_select_fusion), calls=%async_computation.1 | async-start | bytes 33554432 | tf_op jit(solution)/shard_map/all_to_all | solution.py:73
  59.7 500.1 %all-gather.5.cloned.1.call-start = ((), (), s32[]{:S(2)}) async-start(), calls=%async_computation.3 | async-start | bytes 8650752 | tf_op jit(solution)/shard_map/all_gather | solution.py:101
  60.4 563.0 %all-gather.3.cloned.1.call-start = ((), (), s32[]{:S(2)}) async-start(), calls=%async_computation.2 | async-start | bytes 7077888 | tf_op jit(solution)/shard_map/all_gather | solution.py:98
  60.5 423.3 %collective-permute-start = (bf16[63,512]{1,0:T(8,128)(2,1)S(1)}, bf16[63,512]{1,0:T(8,128)(2,1)S(1)}, u32[]{:S(2)}, u32[]{:S(2)}) collective-permute-start(bf16[63,512]{1,0:T(8,128)(2,1)S(1)} %slice.19), channel_id=1, source_target_pairs={{8,0},{16,8},{24,16},{32,24},{40,32},{48,40},{56,48},{64,56},{72,6... | collective-permute-start | bytes 193544 | tf_op jit(solution)/shard_map/ppermute | solution.py:13
  555.7 67.7 %copy-start.2 = (bf16[768,1024]{1,0:T(8,128)(2,1)S(1)}, bf16[768,1024]{1,0:T(8,128)(2,1)}, u32[]{:S(2)}) copy-start(bf16[768,1024]{1,0:T(8,128)(2,1)} %param.7) | copy-start | bytes 4718596
  555.9 2.7 collective-permute-start.1
Sparse Core Ops, SparseCore 0:
  63.1 223.1 all-gather.4
  559.8 63.5 all-gather.2
where the time goes:
time: 643 us; the launch traced here: 642 us
  waiting for transfers between devices  493 us (77%)
  local copies, waits for them, and re-layouts  49.5 us (8%)
  other arithmetic  35.2 us (5%)
  matrix products  22.1 us (3%)
  blocking collectives  20.5 us (3%)
  between operations  13.6 us (2%)
  starting transfers between devices  8.27 us (1%)
    ppermute x2, waiting for transfers between devices, from_behind(): lax.ppermute(value, axis, [(source, source + steps) for source in range(l...  422 us
    all_gather x1, waiting for transfers between devices, shards(): every_head = lax.all_gather(placed, 'head', axis=1, tiled=True)  63.7 us
    all_to_all x1, blocking collectives, shards(): lax.all_to_all(wanted.reshape(seq_count, capacity), 'seq', split_axis=0,...  20.5 us
    gather x2, local copies, waits for them, and re-layouts, shards(): jnp.take(arrived.reshape((slot_total,) + entry_shape), target, axis=0)  18.9 us
    select_n x2, other arithmetic, shards(): picked = jnp.take(nbr_kv, slot_ids.reshape(-1), axis=0)  14.2 us
  transfers between devices with their start and end apart: 5, of which 4 were waited for; matrix products, arithmetic and copies ran while one was open for 10% of the time, Pallas kernels for 0%

commit v1 on v0

v1 whole, which is shorter than its diff:
```python
import jax
import jax.numpy as jnp
from jax import lax
from jax.experimental import pallas as pl
from jax.experimental.pallas import tpu as pltpu
from jax.sharding import PartitionSpec as P

HDIM = 128
BLOCK = 64
KEPT = BLOCK - 1
STAT_ROWS = 8
NAMED = 2
VMEM = pl.BlockSpec(memory_space=pltpu.VMEM)


def call(kernel, name, scalars, inputs, outputs, limit, flops=0, moved=0):
    return pl.pallas_call(
        kernel,
        grid_spec=pltpu.PrefetchScalarGridSpec(
            num_scalar_prefetch=len(scalars),
            grid=(),
            in_specs=[VMEM] * len(inputs),
            out_specs=[VMEM] * len(outputs),
        ),
        out_shape=outputs,
        compiler_params=pltpu.CompilerParams(vmem_limit_bytes=limit << 20),
        cost_estimate=pl.CostEstimate(flops=flops, bytes_accessed=moved, transcendentals=0),
        name=name,
    )(*scalars, *inputs)


def like(shape):
    return jax.ShapeDtypeStruct(shape, jnp.bfloat16)


def spread(value):
    high = value.astype(jnp.bfloat16).astype(jnp.float32)
    rest = value - high
    middle = rest.astype(jnp.bfloat16).astype(jnp.float32)
    return jnp.concatenate([high, middle, rest - middle], axis=1)


def send_kernel(target, query_ref, next_ref, out_ref):
    blocks, rows, width = query_ref.shape
    kept = lax.broadcasted_iota(jnp.int32, (rows, width), 0) < rows - 1
    for block in range(blocks):
        after = query_ref[block + 1] if block + 1 < blocks else next_ref[...]
        turned = jnp.where(kept, after, query_ref[block])
        for index in range(2):
            out_ref[target[2 * block + index]] = turned


def attend_kernel(order, slots, count, query_ref, kv_ref, out_ref):
    width = query_ref.shape[2]
    heads = width // HDIM
    lane = lax.broadcasted_iota(jnp.int32, (BLOCK, HDIM), 1)

    def one(index, carry):
        place = order[index]
        slot = slots[place]
        stats = jnp.zeros((BLOCK, HDIM), jnp.float32)
        for head in range(heads):
            cols = slice(head * HDIM, (head + 1) * HDIM)
            scores = lax.dot_general(
                query_ref[place, :, cols],
                kv_ref[slot, 0, :, cols],
                (((1,), (1,)), ((), ())),
                preferred_element_type=jnp.float32,
            ) * HDIM ** (-0.5)
            top = jnp.max(scores, axis=1, keepdims=True)
            weights = jnp.exp(scores - top)
            total = jnp.sum(weights, axis=1, keepdims=True)
            blended = jnp.dot(
                weights.astype(jnp.bfloat16),
                kv_ref[slot, 1, :, cols],
                preferred_element_type=jnp.float32,
            )
            out_ref[place, :BLOCK, cols] = (blended / total).astype(jnp.bfloat16)
            stats = jnp.where(lane == head, top, stats)
            stats = jnp.where(lane == heads + head, total, stats)
        pieces = spread(stats.T[:STAT_ROWS])
        filler = jnp.zeros((STAT_ROWS, width - 3 * BLOCK), jnp.float32)
        out_ref[place, BLOCK:, :] = jnp.concatenate([pieces, filler], axis=1).astype(jnp.bfloat16)
        return carry

    lax.fori_loop(0, count[0], one, 0)


def combine_kernel(target, parts_ref, out_ref, last_ref):
    blocks, rows, width = out_ref.shape
    heads = width // HDIM
    kept = lax.broadcasted_iota(jnp.int32, (rows, width), 0) < rows - 1

    def joined(block):
        tops, sums = [], []
        places = [target[2 * block + index] for index in range(2)]
        for place in places:
            pieces = parts_ref[place, rows:, :].astype(jnp.float32)
            stats = pieces[:, :rows] + pieces[:, rows : 2 * rows] + pieces[:, 2 * rows : 3 * rows]
            tops.append(stats[:heads])
            sums.append(stats[heads : 2 * heads])
        joint = jnp.maximum(tops[0], tops[1])
        factors = [jnp.exp(top - joint) * total for top, total in zip(tops, sums)]
        whole = factors[0] + factors[1]
        shares = jnp.concatenate([factors[0] / whole, factors[1] / whole], axis=0)
        shares = jnp.concatenate([shares] * (HDIM // (2 * heads)), axis=0)
        columns = jnp.concatenate([shares, shares], axis=1).T[:rows]
        merged = []
        for head in range(heads):
            cols = slice(head * HDIM, (head + 1) * HDIM)
            first, second = (parts_ref[place, :rows, cols].astype(jnp.float32) for place in places)
            merged.append(columns[:, head : head + 1] * first + columns[:, heads + head : heads + head + 1] * second)
        return jnp.concatenate(merged, axis=1)

    before = joined(0)
    out_ref[0] = before.astype(jnp.bfloat16)
    for block in range(1, blocks):
        now = joined(block)
        out_ref[block] = jnp.where(kept, before, now).astype(jnp.bfloat16)
        before = now
    last_ref[...] = before.astype(jnp.bfloat16)


def swap(value):
    return lax.all_to_all(value, "seq", split_axis=0, concat_axis=0, tiled=True)


def shards(queries, residual, nbr_kv, nbr_owner, nbr_slot, out_weight):
    tok_rows, width = queries.shape
    blocks = tok_rows // BLOCK
    seq_count = lax.axis_size("seq")
    places = seq_count * NAMED
    all_weight = lax.all_gather(out_weight, "seq", axis=0, tiled=True)

    owners = nbr_owner.reshape(-1)
    position = jnp.arange(owners.shape[0], dtype=jnp.int32)
    earlier = (owners[:, None] == owners[None, :]) & (position[None, :] < position[:, None])
    target = owners * NAMED + jnp.sum(earlier.astype(jnp.int32), axis=1)
    place = jnp.arange(places, dtype=jnp.int32)
    match = (place[:, None] == target[None, :]).astype(jnp.int32)
    asked = jnp.sum(match * (nbr_slot.reshape(-1) + 1)[None, :], axis=1)
    heard = swap(asked.reshape(seq_count, NAMED)).reshape(-1)

    first_next = lax.ppermute(queries[:BLOCK], "seq", [(s, s - 1) for s in range(1, seq_count)])
    chunks = queries.reshape(blocks, BLOCK, width)
    (sent,) = call(send_kernel, "send", [target], [chunks, first_next], [like((places, BLOCK, width))], 16)
    arrived = swap(sent)

    takes = (heard > 0).astype(jnp.int32)
    rank = jnp.cumsum(takes) - takes
    order = jnp.sum(jnp.where((takes[None, :] > 0) & (rank[None, :] == place[:, None]), place[None, :], 0), axis=1)
    (partial,) = call(
        attend_kernel,
        "attend",
        [order, jnp.maximum(heard - 1, 0), jnp.sum(takes).reshape(1)],
        [arrived, nbr_kv],
        [like((places, BLOCK + STAT_ROWS, width))],
        32,
    )
    moved, last = call(
        combine_kernel, "combine", [target], [swap(partial)], [like((blocks, BLOCK, width)), like((BLOCK, width))], 32
    )
    carried = lax.ppermute(last, "seq", [(s, s + 1) for s in range(seq_count - 1)])
    chunk = lax.broadcasted_iota(jnp.int32, (blocks, 1, 1), 0)
    row = lax.broadcasted_iota(jnp.int32, (1, BLOCK, 1), 1)
    placed = jnp.where((chunk == 0) & (row < KEPT), carried[None], moved).reshape(tok_rows, width)
    every_head = lax.all_gather(placed, "head", axis=1, tiled=True)
    projected = jnp.dot(every_head, all_weight, preferred_element_type=jnp.float32)
    return (residual.astype(jnp.float32) + projected).astype(jnp.bfloat16)


def solution(mesh):
    return jax.shard_map(
        shards,
        mesh=mesh,
        in_specs=(
            P("seq", "head"),
            P("seq", "head"),
            P("seq", None, None, "head"),
            P("seq", None),
            P("seq", None),
            P("seq", "head"),
        ),
        out_specs=P("seq", "head"),
        check_vma=False,
    )
```

time: 643 us -> 421 us (0.65)
  waiting for transfers between devices: 493 us -> 262 us
  starting transfers between devices: 8.27 us -> 83.2 us
  local copies, waits for them, and re-layouts: 49.5 us -> 10.3 us
  Pallas kernels: 0 us -> 33.4 us
  other arithmetic: 35.2 us -> 3.15 us
  blocking collectives: 20.5 us -> 0 us
  matrix products: 22.1 us -> 12.1 us
    ppermute x2, waiting for transfers between devices: 422 us -> 1.24 us  [the longest x1 1.24 us: shards(): lax.ppermute(last, 'seq', [(s, s + 1) for s in range(seq_count - 1)])]
    all_to_all x1 -> x3, waiting for transfers between devices: 6.4 us -> 211 us  [swap(): return lax.all_to_all(value, 'seq', split_axis=0, concat_axis=0, tiled=True)]
    all_to_all x1 -> x3, starting transfers between devices: 5.3 us -> 80.6 us  [swap(): return lax.all_to_all(value, 'seq', split_axis=0, concat_axis=0, tiled=True)]
    pallas_call x0 -> x3, Pallas kernels: none -> 33.4 us  [call(): pl.pallas_call(kernel, grid_spec=pltpu.PrefetchScalarGridSpec(num_scalar_...]
    gather x3 -> x0, local copies, waits for them, and re-layouts: 28.4 us -> none  [the longest x2 18.9 us: shards(): jnp.take(arrived.reshape((slot_total,) + entry_shape), target, axis=0)]
    all_to_all x1 -> x0, blocking collectives: 20.5 us -> none  [shards(): lax.all_to_all(wanted.reshape(seq_count, capacity), 'seq', split_axis=0,...]
    select_n x4 -> x1, other arithmetic: 17.7 us -> 1.05 us  [shards(): jnp.where((chunk == 0) & (row < KEPT), carried[None], moved)]
    all_gather x1, waiting for transfers between devices: 63.7 us -> 49.2 us  [shards(): every_head = lax.all_gather(placed, 'head', axis=1, tiled=True)]
  transfers between devices with their start and end apart: 5 -> 7, of which waited for: 4 -> 5; matrix products, arithmetic and copies ran while one was open for 10% -> 1% of each run, Pallas kernels for 0% -> 8%
where the time goes in v1:
time: 421 us; the launch traced here: 418 us
  waiting for transfers between devices  262 us (62%)
  starting transfers between devices  83.2 us (20%)
  Pallas kernels  33.4 us (8%)
  between operations  13.6 us (3%)
  matrix products  12.1 us (3%)
  local copies, waits for them, and re-layouts  10.3 us (2%)
    all_to_all x3, waiting for transfers between devices, swap(): return lax.all_to_all(value, 'seq', split_axis=0, concat_axis=0, tiled=True)  211 us
    all_to_all x3, starting transfers between devices, swap(): return lax.all_to_all(value, 'seq', split_axis=0, concat_axis=0, tiled=True)  80.6 us
    all_gather x1, waiting for transfers between devices, shards(): every_head = lax.all_gather(placed, 'head', axis=1, tiled=True)  49.2 us
    pallas_call x3, Pallas kernels, call(): pl.pallas_call(kernel, grid_spec=pltpu.PrefetchScalarGridSpec(num_scalar_...  33.4 us
    dot_general x1, matrix products, shards(): jnp.dot(every_head, all_weight, preferred_element_type=jnp.float32)  12.1 us
  transfers between devices with their start and end apart: 7, of which 5 were waited for; matrix products, arithmetic and copies ran while one was open for 1% of the time, Pallas kernels for 8%

profile of v1, /device:TPU:1, one launch (start us, length us, event | category | flops | bytes accessed | tf_op | source)
XLA Modules:
  0.0 417.7 jit_solution(5180622626627021063)
XLA Ops:
  6.5 0.8 slice.3
  7.4 1.3 collective-permute-start
  8.7 0.8 copy.17
  9.4 0.1 reshape.144
  9.5 0.2 convert_reduce_fusion
  9.7 0.7 broadcast_add_fusion
  10.4 0.1 copy.18
  10.5 0.1 add.20
  10.6 0.1 select_reduce_fusion.1
  10.7 0.7 all_to_all.12
  11.4 12.9 %all-to-all-start = ((s32[32,1,2]{2,1,0:T(1,128)}), s32[32,1,2]{2,1,0:T(1,128)S(1)}, u32[]{:S(2)}, u32[]{:S(2)}) async-start(s32[32,1,2]{2,1,0:T(1,128)} %bitcast), calls=%async_computation | async-start | bytes 32768 | tf_op jit(solution)/shard_map/all_to_all | solution.py:125
  24.3 0.0 collective-permute-done.next_ref
  24.3 0.0 copy-start.3
  24.4 1.1 copy-done.3
  25.5 0.6 send.1
  26.1 0.0 copy-start.1
  26.1 1.9 copy-done.1
  28.1 4.8 %all-to-all-done = s32[32,1,2]{2,1,0:T(1,128)S(1)} async-done(((s32[32,1,2]{2,1,0:T(1,128)}), s32[32,1,2]{2,1,0:T(1,128)S(1)}, u32[]{:S(2)}, u32[]{:S(2)}) %all-to-all-start) | async-done | bytes 288 | tf_op jit(solution)/shard_map/all_to_all | solution.py:125
  32.9 4.9 %all-to-all-start.1 = ((bf16[64,64,512]{2,1,0:T(8,128)(2,1)}), bf16[64,64,512]{2,1,0:T(8,128)(2,1)}, u32[]{:S(2)}, u32[]{:S(2)}) async-start(bf16[64,64,512]{2,1,0:T(8,128)(2,1)} %copy-done.1), calls=%async_computation.1 | async-start | bytes 8388608 | tf_op jit(solution)/shard_map/all_to_all | solution.py:125
  37.8 0.0 all-gather.5.cloned.1.call-start
  37.8 0.7 all-gather.5.cloned.1.call-update
  38.5 0.7 fusion.3
  39.2 0.1 reshape.149
  39.3 0.1 reshape.151
  39.4 0.1 reduce-window.8
  39.5 0.1 reduce.4
  39.6 0.1 max.6.slots
  39.8 0.1 select_reduce_fusion.order
  39.9 102.9 %all-to-all-done.1.query_ref = bf16[64,64,512]{2,1,0:T(8,128)(2,1)} async-done(((bf16[64,64,512]{2,1,0:T(8,128)(2,1)}), bf16[64,64,512]{2,1,0:T(8,128)(2,1)}, u32[]{:S(2)}, u32[]{:S(2)}) %all-to-all-start.1) | async-done | bytes 4194336 | tf_op jit(solution)/shard_map/all_to_all | solution.py:125
  142.8 0.0 copy-start.2
  142.8 2.2 copy-done.2
  145.0 26.7 %attend.1 = bf16[64,72,512]{2,1,0:T(8,128)(2,1)S(1)} custom-call(s32[64]{0:T(128)S(1)} %select_reduce_fusion.order, s32[64]{0:T(128)S(1)} %max.6.slots, s32[1]{0:T(128)} %bitcast.1.count, bf16[64,64,512]{2,1,0:T(8,128)(2,1)} %all-to-all-done.1.query_ref, bf16[16,2,128,512]{3,2,1,0:T(8,128)(2,1)S(1)} %copy-done.2), custom_call_target="tpu_custom_call" | custom-call | tf_op jit(solution)/shard_map/attend/pallas_call | solution.py:17
  171.7 0.0 copy-start
  171.7 2.1 copy-done
  173.8 62.8 %all-to-all-start.2 = ((bf16[64,72,512]{2,1,0:T(8,128)(2,1)}), bf16[64,72,512]{2,1,0:T(8,128)(2,1)}, u32[]{:S(2)}, u32[]{:S(2)}) async-start(bf16[64,72,512]{2,1,0:T(8,128)(2,1)} %copy-done), calls=%async_computation.2 | async-start | bytes 9437184 | tf_op jit(solution)/shard_map/all_to_all | solution.py:125
  236.6 0.0 copy-start.4
  236.6 0.0 all-gather.3.cloned.1.call-start
  236.6 103.1 %all-to-all-done.2.parts_ref = bf16[64,72,512]{2,1,0:T(8,128)(2,1)} async-done(((bf16[64,72,512]{2,1,0:T(8,128)(2,1)}), bf16[64,72,512]{2,1,0:T(8,128)(2,1)}, u32[]{:S(2)}, u32[]{:S(2)}) %all-to-all-start.2) | async-done | bytes 4718624 | tf_op jit(solution)/shard_map/all_to_all | solution.py:125
  339.8 6.1 %combine.1 = (bf16[12,64,512]{2,1,0:T(8,128)(2,1)S(1)}, bf16[64,512]{1,0:T(8,128)(2,1)S(1)}) custom-call(s32[24]{0:T(128)S(1)} %multiply_add_fusion.target, bf16[64,72,512]{2,1,0:T(8,128)(2,1)} %all-to-all-done.2.parts_ref), custom_call_target="tpu_custom_call" | custom-call | tf_op jit(solution)/shard_map/combine/pallas_call | solution.py:17
  345.8 1.3 collective-permute-start.1
  347.1 0.1 broadcast_and_fusion
  347.2 1.2 collective-permute-done.1
  348.5 1.1 broadcast_select_fusion
  349.5 0.0 all-gather.3.cloned.1.call-update
  349.5 0.0 all-gather.5.cloned.1.call-done
  349.6 49.2 %all-gather.3.cloned.1.call-done = bf16[768,4096]{1,0:T(8,128)(2,1)} async-done(((bf16[768,512]{1,0:T(8,128)(2,1)}), bf16[768,4096]{1,0:T(8,128)(2,1)}) %all-gather.3.cloned.1.call-update) | async-done | bytes 6291472 | tf_op jit(solution)/shard_map/all_gather | solution.py:167
  398.8 0.0 copy-done.4
  398.8 12.1 %add_convert_fusion = bf16[768,1024]{1,0:T(8,128)(2,1)} fusion(bf16[768,1024]{1,0:T(8,128)(2,1)S(1)} %copy-done.4, bf16[768,4096]{1,0:T(8,128)(2,1)} %all-gather.3.cloned.1.call-done, bf16[4096,1024]{1,0:T(8,128)(2,1)} %all-gather.5.cloned.1.call-done), kind=kOutput, calls=%fused_computation | convolution fusion | flops 6444810240 | bytes 17825792 | tf_op jit(solution)/shard_map/dot_general | solution.py:168
  (6 shorter events, 0.0 us)
Async XLA Ops:
  7.4 17.0 %collective-permute-start = (bf16[64,512]{1,0:T(8,128)(2,1)S(1)}, bf16[64,512]{1,0:T(8,128)(2,1)S(1)}, u32[]{:S(2)}, u32[]{:S(2)}) collective-permute-start(bf16[64,512]{1,0:T(8,128)(2,1)S(1)} %slice.3), channel_id=1, source_target_pairs={{8,0},{16,8},{24,16},{32,24},{40,32},{48,40},{56,48},{64,56},{72,6... | collective-permute-start | bytes 196616 | tf_op jit(solution)/shard_map/ppermute | solution.py:144
  11.4 21.5 %all-to-all-start = ((s32[32,1,2]{2,1,0:T(1,128)}), s32[32,1,2]{2,1,0:T(1,128)S(1)}, u32[]{:S(2)}, u32[]{:S(2)}) async-start(s32[32,1,2]{2,1,0:T(1,128)} %bitcast), calls=%async_computation | async-start | bytes 32768 | tf_op jit(solution)/shard_map/all_to_all | solution.py:125
  24.3 1.1 copy-start.3
  26.1 2.0 copy-start.1
  32.9 109.9 %all-to-all-start.1 = ((bf16[64,64,512]{2,1,0:T(8,128)(2,1)}), bf16[64,64,512]{2,1,0:T(8,128)(2,1)}, u32[]{:S(2)}, u32[]{:S(2)}) async-start(bf16[64,64,512]{2,1,0:T(8,128)(2,1)} %copy-done.1), calls=%async_computation.1 | async-start | bytes 8388608 | tf_op jit(solution)/shard_map/all_to_all | solution.py:125
  37.8 311.8 %all-gather.5.cloned.1.call-start = ((), (), s32[]{:S(2)}) async-start(), calls=%async_computation.4 | async-start | bytes 8650752 | tf_op jit(solution)/shard_map/all_gather | solution.py:133
  142.8 2.2 copy-start.2
  171.7 2.1 copy-start
  173.8 166.0 %all-to-all-start.2 = ((bf16[64,72,512]{2,1,0:T(8,128)(2,1)}), bf16[64,72,512]{2,1,0:T(8,128)(2,1)}, u32[]{:S(2)}, u32[]{:S(2)}) async-start(bf16[64,72,512]{2,1,0:T(8,128)(2,1)} %copy-done), calls=%async_computation.2 | async-start | bytes 9437184 | tf_op jit(solution)/shard_map/all_to_all | solution.py:125
  236.6 162.2 %copy-start.4 = (bf16[768,1024]{1,0:T(8,128)(2,1)S(1)}, bf16[768,1024]{1,0:T(8,128)(2,1)}, u32[]{:S(2)}) copy-start(bf16[768,1024]{1,0:T(8,128)(2,1)} %param.7) | copy-start | bytes 4718596
  236.6 162.2 %all-gather.3.cloned.1.call-start = ((), (), s32[]{:S(2)}) async-start(), calls=%async_computation.3 | async-start | bytes 7077888 | tf_op jit(solution)/shard_map/all_gather | solution.py:167
  345.8 2.6 collective-permute-start.1
Sparse Core Ops, SparseCore 0:
  41.2 139.9 all-gather.4
  349.7 49.0 all-gather.2

commit v2 on v1

v2 whole, which is shorter than its diff:
```python
import jax
import jax.numpy as jnp
from jax import lax
from jax.experimental import pallas as pl
from jax.experimental.pallas import tpu as pltpu
from jax.sharding import PartitionSpec as P

HDIM = 128
BLOCK = 64
KEPT = BLOCK - 1
STAT_ROWS = 8
NAMED = 2
AT_ONCE = 2
VMEM = pl.BlockSpec(memory_space=pltpu.VMEM)


def call(kernel, name, scalars, inputs, outputs, limit, scratch=()):
    return pl.pallas_call(
        kernel,
        grid_spec=pltpu.PrefetchScalarGridSpec(
            num_scalar_prefetch=len(scalars),
            grid=(),
            in_specs=[VMEM] * len(inputs),
            out_specs=[VMEM] * len(outputs),
            scratch_shapes=scratch,
        ),
        out_shape=outputs,
        compiler_params=pltpu.CompilerParams(vmem_limit_bytes=limit << 20),
        name=name,
    )(*scalars, *inputs)


def like(shape):
    return jax.ShapeDtypeStruct(shape, jnp.bfloat16)


def spread(value):
    high = value.astype(jnp.bfloat16).astype(jnp.float32)
    rest = value - high
    middle = rest.astype(jnp.bfloat16).astype(jnp.float32)
    return jnp.concatenate([high, middle, rest - middle], axis=1)


def send_kernel(target, info, query_ref, next_ref, out_ref):
    blocks, rows, width = query_ref.shape
    kept = lax.broadcasted_iota(jnp.int32, (rows, width), 0) < rows - 1
    lane = lax.broadcasted_iota(jnp.int32, (STAT_ROWS, width), 1)
    for owner in range(out_ref.shape[0]):
        ids = jnp.where(lane == 0, info[NAMED * owner], 0) + jnp.where(lane == 1, info[NAMED * owner + 1], 0)
        out_ref[owner, NAMED * rows :, :] = ids.astype(jnp.float32).astype(jnp.bfloat16)
    for block in range(blocks):
        after = query_ref[block + 1] if block + 1 < blocks else next_ref[...]
        turned = jnp.where(kept, after, query_ref[block])
        for index in range(2):
            place = target[2 * block + index]
            start = pl.multiple_of(lax.rem(place, NAMED) * rows, rows)
            out_ref[lax.div(place, NAMED), pl.ds(start, rows), :] = turned


def attend_kernel(heard, query_ref, kv_ref, out_ref, listed):
    places = heard.shape[0]
    width = query_ref.shape[2]
    pair = 2 * HDIM
    zero = jnp.zeros((BLOCK, HDIM), jnp.bfloat16)

    def note(place, count):
        @pl.when(heard[place] > 0)
        def _():
            listed[count] = place

        return count + (heard[place] > 0).astype(jnp.int32)

    count = lax.fori_loop(0, places, note, 0)

    def some(index, carry):
        work = []
        for other in range(AT_ONCE):
            place = listed[jnp.minimum(index * AT_ONCE + other, count - 1)]
            slot = heard[place] - 1
            start = pl.multiple_of(lax.rem(place, NAMED) * BLOCK, BLOCK)
            for first in range(0, width, pair):
                work.append((place, slot, lax.div(place, NAMED), start, first))
        scores = []
        for place, slot, source, start, first in work:
            left = query_ref[source, pl.ds(start, BLOCK), first : first + HDIM]
            right = query_ref[source, pl.ds(start, BLOCK), first + HDIM : first + pair]
            both = jnp.concatenate(
                [jnp.concatenate([left, zero], axis=1), jnp.concatenate([zero, right], axis=1)], axis=0
            )
            scores.append(
                lax.dot_general(
                    kv_ref[slot, 0, :, first : first + pair],
                    both,
                    (((1,), (1,)), ((), ())),
                    preferred_element_type=jnp.float32,
                )
                * HDIM ** (-0.5)
            )
        tops = [jnp.max(score, axis=0, keepdims=True) for score in scores]
        weights = [jnp.exp(score - top) for score, top in zip(scores, tops)]
        totals = [jnp.sum(weight, axis=0, keepdims=True) for weight in weights]
        shares = [(weight * (1.0 / total)).astype(jnp.bfloat16) for weight, total in zip(weights, totals)]
        for (place, slot, source, start, first), share in zip(work, shares):
            blended = lax.dot_general(
                share,
                kv_ref[slot, 1, :, first : first + pair],
                (((0,), (0,)), ((), ())),
                preferred_element_type=jnp.float32,
            )
            out_ref[place, :BLOCK, first : first + HDIM] = blended[:BLOCK, :HDIM].astype(jnp.bfloat16)
            out_ref[place, :BLOCK, first + HDIM : first + pair] = blended[BLOCK:, HDIM:].astype(jnp.bfloat16)
        pairs = width // pair
        for other in range(AT_ONCE):
            own = slice(other * pairs, (other + 1) * pairs)
            rows = jnp.concatenate(
                tops[own] + totals[own] + [jnp.zeros((STAT_ROWS - 2 * pairs, HDIM), jnp.float32)], axis=0
            )
            pieces = [spread(rows), jnp.zeros((STAT_ROWS, width - 3 * HDIM), jnp.float32)]
            out_ref[work[other * pairs][0], BLOCK:, :] = jnp.concatenate(pieces, axis=1).astype(jnp.bfloat16)
        return carry

    lax.fori_loop(0, lax.div(count + AT_ONCE - 1, AT_ONCE), some, 0)


def combine_kernel(target, parts_ref, out_ref, last_ref):
    blocks, rows, width = out_ref.shape
    pairs = width // (2 * HDIM)
    kept = lax.broadcasted_iota(jnp.int32, (rows, width), 0) < rows - 1

    def joined(block):
        tops, sums = [], []
        places = [target[2 * block + index] for index in range(2)]
        for place in places:
            pieces = parts_ref[place, rows:, :].astype(jnp.float32)
            stats = pieces[:, :HDIM] + pieces[:, HDIM : 2 * HDIM] + pieces[:, 2 * HDIM : 3 * HDIM]
            tops.append(stats[:pairs])
            sums.append(stats[pairs : 2 * pairs])
        joint = jnp.maximum(tops[0], tops[1])
        factors = [jnp.exp(top - joint) * total for top, total in zip(tops, sums)]
        whole = factors[0] + factors[1]
        shares = jnp.concatenate([factors[0] / whole, factors[1] / whole], axis=0)
        columns = jnp.concatenate([shares] * (HDIM // (2 * pairs)), axis=0).T
        merged = []
        for head in range(2 * pairs):
            cols = slice(head * HDIM, (head + 1) * HDIM)
            own = slice(head % 2 * rows, head % 2 * rows + rows)
            first, second = (parts_ref[place, :rows, cols].astype(jnp.float32) for place in places)
            at = head // 2
            merged.append(columns[own, at : at + 1] * first + columns[own, pairs + at : pairs + at + 1] * second)
        return jnp.concatenate(merged, axis=1)

    before = joined(0)
    out_ref[0] = before.astype(jnp.bfloat16)
    for block in range(1, blocks):
        now = joined(block)
        out_ref[block] = jnp.where(kept, before, now).astype(jnp.bfloat16)
        before = now
    last_ref[...] = before.astype(jnp.bfloat16)


def early_kernel(_, *refs):
    *refs, out_ref = refs
    count = len(refs) // 2
    total = None
    for own, weight in zip(refs[:count], refs[count:]):
        product = jnp.dot(own[...], weight[...], preferred_element_type=jnp.float32)
        total = product if total is None else total + product
    out_ref[...] = total


def late_kernel(_, sum_ref, residual_ref, *refs):
    *refs, out_ref = refs
    count = len(refs) // 3
    half = out_ref.shape[0] // 2
    for part in range(2):
        rows = slice(part * half, (part + 1) * half)
        total = sum_ref[rows, :] + residual_ref[rows, :].astype(jnp.float32)
        for own, weight in zip(refs[part * count : (part + 1) * count], refs[2 * count :]):
            total = total + jnp.dot(own[...], weight[...], preferred_element_type=jnp.float32)
        out_ref[rows, :] = total.astype(jnp.bfloat16)


TILE = 256


def project(kernel, name, heads, tiled, whole, weight, out_type):
    rows, features = tiled[0].shape if tiled else (whole[0].shape[0], weight.shape[1])
    depth = whole[0].shape[1]
    count = heads.shape[0]
    specs = [pl.BlockSpec((rows, TILE), lambda j, at: (0, j)) for _ in tiled]
    specs += [pl.BlockSpec(value.shape, lambda j, at: (0, 0)) for value in whole]
    specs += [pl.BlockSpec((depth, TILE), lambda j, at, i=i: (at[i], j)) for i in range(count)]
    return pl.pallas_call(
        kernel,
        grid_spec=pltpu.PrefetchScalarGridSpec(
            num_scalar_prefetch=1,
            grid=(features // TILE,),
            in_specs=specs,
            out_specs=pl.BlockSpec((rows, TILE), lambda j, at: (0, j)),
        ),
        out_shape=jax.ShapeDtypeStruct((rows, features), out_type),
        compiler_params=pltpu.CompilerParams(vmem_limit_bytes=40 << 20),
        cost_estimate=pl.CostEstimate(
            flops=2 * rows * features * depth * count, bytes_accessed=4 * rows * features, transcendentals=0
        ),
        name=name,
    )(heads, *tiled, *whole, *([weight] * count))


def swap(value):
    return lax.all_to_all(value, "seq", split_axis=0, concat_axis=0, tiled=True)


def shards(queries, residual, nbr_kv, nbr_owner, nbr_slot, out_weight):
    tok_rows, width = queries.shape
    blocks = tok_rows // BLOCK
    seq_count = lax.axis_size("seq")
    places = seq_count * NAMED
    all_weight = lax.all_gather(out_weight, "seq", axis=0, tiled=True)

    owners = nbr_owner.reshape(-1)
    position = jnp.arange(owners.shape[0], dtype=jnp.int32)
    earlier = (owners[:, None] == owners[None, :]) & (position[None, :] < position[:, None])
    target = owners * NAMED + jnp.sum(earlier.astype(jnp.int32), axis=1)
    place = jnp.arange(places, dtype=jnp.int32)
    match = (place[:, None] == target[None, :]).astype(jnp.int32)
    asked = jnp.sum(match * (nbr_slot.reshape(-1) + 1)[None, :], axis=1)

    first_next = lax.ppermute(queries[:BLOCK], "seq", [(s, s - 1) for s in range(1, seq_count)])
    chunks = queries.reshape(blocks, BLOCK, width)
    pack = like((seq_count, NAMED * BLOCK + STAT_ROWS, width))
    (sent,) = call(send_kernel, "send", [target, asked], [chunks, first_next], [pack], 16)
    arrived = swap(sent)
    heard = arrived[:, NAMED * BLOCK, :NAMED].astype(jnp.int32).reshape(-1)
    (partial,) = call(
        attend_kernel,
        "attend",
        [heard],
        [arrived, nbr_kv],
        [like((places, BLOCK + STAT_ROWS, width))],
        40,
        [pltpu.SMEM((places,), jnp.int32)],
    )
    moved, last = call(
        combine_kernel, "combine", [target], [swap(partial)], [like((blocks, BLOCK, width)), like((BLOCK, width))], 32
    )
    carried = lax.ppermute(last, "seq", [(s, s + 1) for s in range(seq_count - 1)])
    chunk = lax.broadcasted_iota(jnp.int32, (blocks, 1, 1), 0)
    row = lax.broadcasted_iota(jnp.int32, (1, BLOCK, 1), 1)
    placed = jnp.where((chunk == 0) & (row < KEPT), carried[None], moved).reshape(tok_rows, width)
    return project_rows(placed, all_weight, residual)


def project_rows(placed, all_weight, residual):
    head_count = lax.axis_size("head")
    chips = head_count // 2
    half = placed.shape[0] // 2
    me = lax.axis_index("head")
    chip, core = me // 2, me % 2

    def along(value, step):
        return lax.ppermute(value, "head", [(h, (h + 2 * step) % head_count) for h in range(head_count)])

    def across(value):
        return lax.ppermute(value, "head", [(h, h ^ 1) for h in range(head_count)])

    def name(step, other):
        return (chip + step) % chips * 2 + (core + other) % 2

    up, down = along(placed, 1), along(placed, -1)
    far_up, far_down = along(up[:half], 1), along(down[half:], -1)
    pieces = [placed, across(placed), up, across(up), down, across(down)]
    heads = jnp.stack([name(step, other) for step in (0, -1, 1) for other in (0, 1)])
    total = project(early_kernel, "early", heads, [], pieces, all_weight, jnp.float32)
    late = [far_up, across(far_up), far_down, across(far_down)]
    heads = jnp.stack([name(2, 0), name(2, 1)])
    return project(late_kernel, "late", heads, [total, residual], late, all_weight, jnp.bfloat16)


def solution(mesh):
    return jax.shard_map(
        shards,
        mesh=mesh,
        in_specs=(
            P("seq", "head"),
            P("seq", "head"),
            P("seq", None, None, "head"),
            P("seq", None),
            P("seq", None),
            P("seq", "head"),
        ),
        out_specs=P("seq", "head"),
        check_vma=False,
    )
```

time: 421 us -> 356 us (0.85)
  starting transfers between devices: 83.2 us -> 58.2 us
  waiting for transfers between devices: 262 us -> 241 us
  matrix products: 12.1 us -> 0 us
  Pallas kernels: 33.4 us -> 27.5 us
    all_gather x1 -> x0, waiting for transfers between devices: 49.2 us -> none  [shards(): every_head = lax.all_gather(placed, 'head', axis=1, tiled=True)]
    all_to_all x3 -> x2, starting transfers between devices: 80.6 us -> 39 us  [swap(): return lax.all_to_all(value, 'seq', split_axis=0, concat_axis=0, tiled=True)]
    pallas_call x3, Pallas kernels: 33.4 us -> 12.9 us  [call(): pl.pallas_call(kernel, grid_spec=pltpu.PrefetchScalarGridSpec(num_scalar_...]
    ppermute x0 -> x9, waiting for transfers between devices: none -> 20.2 us  [the longest x4 20.2 us: along(): lax.ppermute(value, 'head', [(h, (h + 2 * step) % head_count) for h in ra...]
    ppermute x0 -> x9, starting transfers between devices: none -> 16.6 us  [the longest x4 8.59 us: along(): lax.ppermute(value, 'head', [(h, (h + 2 * step) % head_count) for h in ra...]
    pallas_call x0 -> x2, Pallas kernels: none -> 14.6 us  [project(): pl.pallas_call(kernel, grid_spec=pltpu.PrefetchScalarGridSpec(num_scalar_...]
    dot_general x1 -> x0, matrix products: 12.1 us -> none  [shards(): jnp.dot(every_head, all_weight, preferred_element_type=jnp.float32)]
    all_to_all x3 -> x2, waiting for transfers between devices: 211 us -> 216 us  [swap(): return lax.all_to_all(value, 'seq', split_axis=0, concat_axis=0, tiled=True)]
  transfers between devices with their start and end apart: 7 -> 14, of which waited for: 5 -> 6; matrix products, arithmetic and copies ran while one was open for 1% -> 1% of each run, Pallas kernels for 8% -> 6%
where the time goes in v2:
time: 356 us; the launch traced here: 354 us
  waiting for transfers between devices  241 us (68%)
  starting transfers between devices  58.2 us (16%)
  Pallas kernels  27.5 us (8%)
  between operations  13.6 us (4%)
  local copies, waits for them, and re-layouts  11.1 us (3%)
    all_to_all x2, waiting for transfers between devices, swap(): return lax.all_to_all(value, 'seq', split_axis=0, concat_axis=0, tiled=True)  216 us
    all_to_all x2, starting transfers between devices, swap(): return lax.all_to_all(value, 'seq', split_axis=0, concat_axis=0, tiled=True)  39 us
    ppermute x4, waiting for transfers between devices, along(): lax.ppermute(value, 'head', [(h, (h + 2 * step) % head_count) for h in ra...  20.2 us
    pallas_call x2, Pallas kernels, project(): pl.pallas_call(kernel, grid_spec=pltpu.PrefetchScalarGridSpec(num_scalar_...  14.6 us
    pallas_call x3, Pallas kernels, call(): pl.pallas_call(kernel, grid_spec=pltpu.PrefetchScalarGridSpec(num_scalar_...  12.9 us
    ppermute x4, starting transfers between devices, along(): lax.ppermute(value, 'head', [(h, (h + 2 * step) % head_count) for h in ra...  8.59 us
    unnamed x11, local copies, waits for them, and re-layouts  8.21 us
    ppermute x5, starting transfers between devices, across(): return lax.ppermute(value, 'head', [(h, h ^ 1) for h in range(head_count)])  7.97 us
  transfers between devices with their start and end apart: 14, of which 6 were waited for; matrix products, arithmetic and copies ran while one was open for 1% of the time, Pallas kernels for 6%

profile of v2, /device:TPU:1, one launch (start us, length us, event | category | flops | bytes accessed | tf_op | source)
XLA Modules:
  0.0 353.9 jit_solution(12556855731015975017)
XLA Ops:
  6.5 0.8 slice.12
  7.4 1.3 collective-permute-start
  8.7 0.8 copy.11
  9.4 0.1 reshape.74
  9.5 0.2 convert_reduce_fusion
  9.7 0.7 broadcast_add_fusion
  10.4 0.1 copy.12
  10.5 0.1 add.109
  10.6 0.1 select_reduce_fusion.info
  10.7 2.7 collective-permute-done.next_ref
  13.4 1.1 copy-done.4
  14.5 0.7 send.1
  15.2 2.0 copy-done.1
  17.2 11.9 %all-to-all-start = ((bf16[32,136,512]{2,1,0:T(8,128)(2,1)}), bf16[32,136,512]{2,1,0:T(8,128)(2,1)}, u32[]{:S(2)}, u32[]{:S(2)}) async-start(bf16[32,136,512]{2,1,0:T(8,128)(2,1)} %copy-done.1), calls=%async_computation | async-start | bytes 8912896 | tf_op jit(solution)/shard_map/all_to_all | solution.py:211
  29.2 0.0 all-gather.2.cloned.1.call-start
  29.2 0.7 all-gather.2.cloned.1.call-update
  29.9 112.0 %all-to-all-done.query_ref = bf16[32,136,512]{2,1,0:T(8,128)(2,1)} async-done(((bf16[32,136,512]{2,1,0:T(8,128)(2,1)}), bf16[32,136,512]{2,1,0:T(8,128)(2,1)}, u32[]{:S(2)}, u32[]{:S(2)}) %all-to-all-start) | async-done | bytes 4456480 | tf_op jit(solution)/shard_map/all_to_all | solution.py:211
  141.9 0.9 fusion
  142.8 0.1 reshape.77.heard
  142.9 0.0 copy-start.2
  142.9 2.2 copy-done.2
  145.1 8.1 %attend.1 = bf16[64,72,512]{2,1,0:T(8,128)(2,1)S(1)} custom-call(s32[64]{0:T(128)S(1)} %reshape.77.heard, bf16[32,136,512]{2,1,0:T(8,128)(2,1)} %all-to-all-done.query_ref, bf16[16,2,128,512]{3,2,1,0:T(8,128)(2,1)S(1)} %copy-done.2), custom_call_target="tpu_custom_call" | custom-call | tf_op jit(solution)/shard_map/attend/pallas_call | solution.py:18
  153.2 2.1 copy-done
  155.3 27.1 %all-to-all-start.1 = ((bf16[64,72,512]{2,1,0:T(8,128)(2,1)}), bf16[64,72,512]{2,1,0:T(8,128)(2,1)}, u32[]{:S(2)}, u32[]{:S(2)}) async-start(bf16[64,72,512]{2,1,0:T(8,128)(2,1)} %copy-done), calls=%async_computation.1 | async-start | bytes 9437184 | tf_op jit(solution)/shard_map/all_to_all | solution.py:211
  182.4 104.5 %all-to-all-done.1.parts_ref = bf16[64,72,512]{2,1,0:T(8,128)(2,1)} async-done(((bf16[64,72,512]{2,1,0:T(8,128)(2,1)}), bf16[64,72,512]{2,1,0:T(8,128)(2,1)}, u32[]{:S(2)}, u32[]{:S(2)}) %all-to-all-start.1) | async-done | bytes 4718624 | tf_op jit(solution)/shard_map/all_to_all | solution.py:211
  287.0 4.1 %combine.1 = (bf16[12,64,512]{2,1,0:T(8,128)(2,1)S(1)}, bf16[64,512]{1,0:T(8,128)(2,1)S(1)}) custom-call(s32[24]{0:T(128)S(1)} %multiply_add_fusion.target, bf16[64,72,512]{2,1,0:T(8,128)(2,1)} %all-to-all-done.1.parts_ref), custom_call_target="tpu_custom_call" | custom-call | tf_op jit(solution)/shard_map/combine/pallas_call | solution.py:18
  291.0 1.3 collective-permute-start.1
  292.3 0.1 broadcast_and_fusion
  292.4 1.2 collective-permute-done.1
  293.7 0.2 broadcast_select_fusion
  293.8 1.1 collective-permute-start.3
  294.9 4.7 %collective-permute-start.5 = (bf16[768,512]{1,0:T(8,128)(2,1)S(1)}, bf16[768,512]{1,0:T(8,128)(2,1)S(1)}, u32[]{:S(2)}, u32[]{:S(2)}) collective-permute-start(bf16[768,512]{1,0:T(8,128)(2,1)S(1)} %bitcast.11), channel_id=1, source_target_pairs={{0,6},{1,7},{2,0},{3,1},{4,2},{5,3},{6,4},{7,5},{8,14},{9,15},{10,... | collective-permute-start | bytes 2359304 | tf_op jit(solution)/shard_map/ppermute | solution.py:262
  299.7 2.9 collective-permute-start.2
  302.6 12.2 %collective-permute-done.3.refs_2_ = bf16[768,512]{1,0:T(8,128)(2,1)S(1)} collective-permute-done((bf16[768,512]{1,0:T(8,128)(2,1)S(1)}, bf16[768,512]{1,0:T(8,128)(2,1)S(1)}, u32[]{:S(2)}, u32[]{:S(2)}) %collective-permute-start.3) | collective-permute-done | bytes 786464 | tf_op jit(solution)/shard_map/ppermute | solution.py:262
  314.7 3.3 collective-permute-start.4
  318.1 0.0 collective-permute-start.6
  318.1 0.8 slice.17
  318.9 0.9 collective-permute-start.7
  319.7 0.8 slice.18
  320.5 1.9 collective-permute-start.9
  322.4 0.1 stack.39._
  322.5 0.1 pad_add_fusion._
  322.6 8.1 %collective-permute-done.7.refs_0_ = bf16[384,512]{1,0:T(8,128)(2,1)S(1)} collective-permute-done((bf16[384,512]{1,0:T(8,128)(2,1)}, bf16[384,512]{1,0:T(8,128)(2,1)S(1)}, u32[]{:S(2)}, u32[]{:S(2)}) %collective-permute-start.7) | collective-permute-done | bytes 393248 | tf_op jit(solution)/shard_map/ppermute | solution.py:262
  330.6 1.3 collective-permute-start.8
  331.9 0.5 collective-permute-start.10
  332.4 0.0 collective-permute-done.2.refs_1_
  332.4 8.7 %early.1.sum_ref = f32[768,1024]{1,0:T(8,128)S(1)} custom-call(s32[6]{0:T(128)S(1)} %stack.39._, bf16[768,512]{1,0:T(8,128)(2,1)S(1)} %bitcast.13, bf16[768,512]{1,0:T(8,128)(2,1)S(1)} %collective-permute-done.2.refs_1_, bf16[768,512]{1,0:T(8,128)(2,1)S(1)} %collective-permute-done.3.refs_2_, bf16[768,512]{1,0:T(8,128)(2,1)} %collective-permute-done.4.refs_3_, ...), custom_call_target="tpu_custom_call" | custom-call | flops 4831838208 | bytes 3145728 | tf_op jit(solution)/shard_map/early/pallas_call | solution.py:193
  341.1 6.0 %late.1 = bf16[768,1024]{1,0:T(8,128)(2,1)} custom-call(s32[2]{0:T(128)S(1)} %pad_add_fusion._, f32[768,1024]{1,0:T(8,128)S(1)} %early.1.sum_ref, bf16[768,1024]{1,0:T(8,128)(2,1)S(1)} %copy-done.3, bf16[384,512]{1,0:T(8,128)(2,1)S(1)} %collective-permute-done.7.refs_0_, bf16[384,512]{1,0:T(8,128)(2,1)} %collective-permute-done.8.refs_1_, ...), custom_call_target="tpu_custom_call" | custom-call | flops 1610612736 | bytes 3145728 | tf_op jit(solution)/shard_map/late/pallas_call | solution.py:193
  (15 shorter events, 0.0 us)
Async XLA Ops:
  7.4 6.0 %collective-permute-start = (bf16[64,512]{1,0:T(8,128)(2,1)S(1)}, bf16[64,512]{1,0:T(8,128)(2,1)S(1)}, u32[]{:S(2)}, u32[]{:S(2)}) collective-permute-start(bf16[64,512]{1,0:T(8,128)(2,1)S(1)} %slice.12), channel_id=1, source_target_pairs={{8,0},{16,8},{24,16},{32,24},{40,32},{48,40},{56,48},{64,56},{72,6... | collective-permute-start | bytes 196616 | tf_op jit(solution)/shard_map/ppermute | solution.py:229
  13.4 1.1 copy-start.4
  15.2 2.0 copy-start.1
  17.2 124.6 %all-to-all-start = ((bf16[32,136,512]{2,1,0:T(8,128)(2,1)}), bf16[32,136,512]{2,1,0:T(8,128)(2,1)}, u32[]{:S(2)}, u32[]{:S(2)}) async-start(bf16[32,136,512]{2,1,0:T(8,128)(2,1)} %copy-done.1), calls=%async_computation | async-start | bytes 8912896 | tf_op jit(solution)/shard_map/all_to_all | solution.py:211
  29.2 303.2 %all-gather.2.cloned.1.call-start = ((), (), s32[]{:S(2)}) async-start(), calls=%async_computation.2 | async-start | bytes 8650752 | tf_op jit(solution)/shard_map/all_gather | solution.py:219
  142.9 2.2 copy-start.2
  153.2 2.1 copy-start
  155.3 131.6 %all-to-all-start.1 = ((bf16[64,72,512]{2,1,0:T(8,128)(2,1)}), bf16[64,72,512]{2,1,0:T(8,128)(2,1)}, u32[]{:S(2)}, u32[]{:S(2)}) async-start(bf16[64,72,512]{2,1,0:T(8,128)(2,1)} %copy-done), calls=%async_computation.1 | async-start | bytes 9437184 | tf_op jit(solution)/shard_map/all_to_all | solution.py:211
  291.0 2.6 collective-permute-start.1
  293.8 20.9 %collective-permute-start.3 = (bf16[768,512]{1,0:T(8,128)(2,1)S(1)}, bf16[768,512]{1,0:T(8,128)(2,1)S(1)}, u32[]{:S(2)}, u32[]{:S(2)}) collective-permute-start(bf16[768,512]{1,0:T(8,128)(2,1)S(1)} %bitcast.10), channel_id=1, source_target_pairs={{0,2},{1,3},{2,4},{3,5},{4,6},{5,7},{6,0},{7,1},{8,10},{9,11},{10,... | collective-permute-start | bytes 2359304 | tf_op jit(solution)/shard_map/ppermute | solution.py:262
  294.9 23.1 %collective-permute-start.5 = (bf16[768,512]{1,0:T(8,128)(2,1)S(1)}, bf16[768,512]{1,0:T(8,128)(2,1)S(1)}, u32[]{:S(2)}, u32[]{:S(2)}) collective-permute-start(bf16[768,512]{1,0:T(8,128)(2,1)S(1)} %bitcast.11), channel_id=1, source_target_pairs={{0,6},{1,7},{2,0},{3,1},{4,2},{5,3},{6,4},{7,5},{8,14},{9,15},{10,... | collective-permute-start | bytes 2359304 | tf_op jit(solution)/shard_map/ppermute | solution.py:262
  299.7 32.7 %collective-permute-start.2 = (bf16[768,512]{1,0:T(8,128)(2,1)S(1)}, bf16[768,512]{1,0:T(8,128)(2,1)S(1)}, u32[]{:S(2)}, u32[]{:S(2)}) collective-permute-start(bf16[768,512]{1,0:T(8,128)(2,1)S(1)} %bitcast.12), channel_id=1, source_target_pairs={{0,1},{1,0},{2,3},{3,2},{4,5},{5,4},{6,7},{7,6},{8,9},{9,8},{10,11... | collective-permute-start | bytes 2359304 | tf_op jit(solution)/shard_map/ppermute | solution.py:265
  314.7 17.6 %collective-permute-start.4 = (bf16[768,512]{1,0:T(8,128)(2,1)S(1)}, bf16[768,512]{1,0:T(8,128)(2,1)}, u32[]{:S(2)}, u32[]{:S(2)}) collective-permute-start(bf16[768,512]{1,0:T(8,128)(2,1)S(1)} %collective-permute-done.3.refs_2_), channel_id=1, source_target_pairs={{0,1},{1,0},{2,3},{3,2},{4,5},{5,4},{6,7},{7,6},{8,9},{9,8},{10,11... | collective-permute-start | bytes 2359304 | tf_op jit(solution)/shard_map/ppermute | solution.py:265
  318.1 14.3 %collective-permute-start.6 = (bf16[768,512]{1,0:T(8,128)(2,1)S(1)}, bf16[768,512]{1,0:T(8,128)(2,1)}, u32[]{:S(2)}, u32[]{:S(2)}) collective-permute-start(bf16[768,512]{1,0:T(8,128)(2,1)S(1)} %collective-permute-done.5.refs_4_), channel_id=1, source_target_pairs={{0,1},{1,0},{2,3},{3,2},{4,5},{5,4},{6,7},{7,6},{8,9},{9,8},{10,11... | collective-permute-start | bytes 2359304 | tf_op jit(solution)/shard_map/ppermute | solution.py:265
  318.9 11.8 %collective-permute-start.7 = (bf16[384,512]{1,0:T(8,128)(2,1)}, bf16[384,512]{1,0:T(8,128)(2,1)S(1)}, u32[]{:S(2)}, u32[]{:S(2)}) collective-permute-start(bf16[384,512]{1,0:T(8,128)(2,1)} %slice.17), channel_id=1, source_target_pairs={{0,2},{1,3},{2,4},{3,5},{4,6},{5,7},{6,0},{7,1},{8,10},{9,11},{10,... | collective-permute-start | bytes 1179656 | tf_op jit(solution)/shard_map/ppermute | solution.py:262
  320.5 11.4 %collective-permute-start.9 = (bf16[384,512]{1,0:T(8,128)(2,1)}, bf16[384,512]{1,0:T(8,128)(2,1)}, u32[]{:S(2)}, u32[]{:S(2)}) collective-permute-start(bf16[384,512]{1,0:T(8,128)(2,1)} %slice.18), channel_id=1, source_target_pairs={{0,6},{1,7},{2,0},{3,1},{4,2},{5,3},{6,4},{7,5},{8,14},{9,15},{10,... | collective-permute-start | bytes 1179656 | tf_op jit(solution)/shard_map/ppermute | solution.py:262
  330.6 10.4 %collective-permute-start.8 = (bf16[384,512]{1,0:T(8,128)(2,1)S(1)}, bf16[384,512]{1,0:T(8,128)(2,1)}, u32[]{:S(2)}, u32[]{:S(2)}) collective-permute-start(bf16[384,512]{1,0:T(8,128)(2,1)S(1)} %collective-permute-done.7.refs_0_), channel_id=1, source_target_pairs={{0,1},{1,0},{2,3},{3,2},{4,5},{5,4},{6,7},{7,6},{8,9},{9,8},{10,11... | collective-permute-start | bytes 1179656 | tf_op jit(solution)/shard_map/ppermute | solution.py:265
  331.9 9.2 %collective-permute-start.10 = (bf16[384,512]{1,0:T(8,128)(2,1)}, bf16[384,512]{1,0:T(8,128)(2,1)}, u32[]{:S(2)}, u32[]{:S(2)}) collective-permute-start(bf16[384,512]{1,0:T(8,128)(2,1)} %collective-permute-done.9.refs_2_), channel_id=1, source_target_pairs={{0,1},{1,0},{2,3},{3,2},{4,5},{5,4},{6,7},{7,6},{8,9},{9,8},{10,11... | collective-permute-start | bytes 1179656 | tf_op jit(solution)/shard_map/ppermute | solution.py:265
  332.3 8.7 %copy-start.3 = (bf16[768,1024]{1,0:T(8,128)(2,1)S(1)}, bf16[768,1024]{1,0:T(8,128)(2,1)}, u32[]{:S(2)}) copy-start(bf16[768,1024]{1,0:T(8,128)(2,1)} %residual_ref.1) | copy-start | bytes 4718596
Sparse Core Ops, SparseCore 0:
  32.6 145.6 all-gather.1
